TPU v7x, 32 devices: a whole 2x2x4 slice. The times are simulated.
32 devices in a mesh: node: 4 (over y, core), seq: 8 (over z, x).
Axes of the slice: x: 2, y: 2, z: 4, core: 2. Of those that a mesh axis runs over, the one named last changes fastest.
Arguments:
- queries: bfloat16 [4096, 4096], P(('node', 'seq')), may hold values from -21 to 21
- keys: bfloat16 [4096, 1024], P(('node', 'seq')), may hold values from -6 to 6
- values: bfloat16 [4096, 1024], P(('node', 'seq')), may hold values from -12 to 12
- routes: int32 [4096, 4], P(('node', 'seq')), may hold values from 0 to 7, all different within a row; in each aligned block of 128 rows (0 to 127, 128 to 255, ...) at most 96 rows name the same one
- gates: bfloat16 [4096, 4], P(('node', 'seq')), may hold values from 0.099609375 to 0.59765625
Outputs:
- expert_rows: bfloat16 [8, 8, 4, 96, 4096], P('node', 'seq')
Inputs may be any that keep to these rules, and one draw needn't show every extreme that they name: `routes`: each row names 4 different experts. In the rows of one device (128 rows, aligned) no expert is named by more than 96 rows, a bound that some block reaches.
All inputs are finite; a program needn't handle non-finite values.
Results may differ from a plain program's by a relative error of at most 0.0057.
Values may be sent and summed in bfloat16 or wider, within the bound.
A program may use at most 64 MiB of HBM per device.

v0:
```python
import jax
import jax.numpy as jnp
from jax import lax
from jax.sharding import PartitionSpec as P

QUERY_HEADS = 32
KEY_VALUE_HEADS = 8
HEAD_SIZE = 128
TOP = 4
EXP_NODE = 2


def softmax_shares(scores, allowed):
    scores = jnp.where(allowed, scores, jnp.float32(-1e30))
    top_score = jnp.max(scores, axis=-1, keepdims=True)
    raised = jnp.exp(scores - top_score)
    return (raised / jnp.sum(raised, axis=-1, keepdims=True)).astype(jnp.bfloat16)


def per_device(queries, keys, values, routes, gates):
    token_rows = queries.shape[0]
    score_scale = HEAD_SIZE ** (-0.5)
    group_members = QUERY_HEADS // KEY_VALUE_HEADS
    query_triple = queries.reshape(token_rows, QUERY_HEADS, HEAD_SIZE)
    key_triple = keys.reshape(token_rows, KEY_VALUE_HEADS, HEAD_SIZE)
    value_triple = values.reshape(token_rows, KEY_VALUE_HEADS, HEAD_SIZE)
    k_full, v_full = (
        lax.all_gather(key_triple, "seq", axis=0, tiled=True),
        lax.all_gather(value_triple, "seq", axis=0, tiled=True),
    )
    span_length = k_full.shape[0]
    key_pos = jnp.arange(span_length, dtype=jnp.int32)
    query_pos = lax.axis_index("seq") * token_rows + jnp.arange(token_rows, dtype=jnp.int32)
    query_groups = jnp.moveaxis(
        query_triple.reshape(token_rows, KEY_VALUE_HEADS, group_members, HEAD_SIZE), 1, 0
    )
    k_moved = jnp.moveaxis(k_full, 1, 0)
    v_moved = jnp.moveaxis(v_full, 1, 0)

    def one_kv(operands):
        q_part, k_part, v_part = operands
        scores = (
            jnp.einsum("tgd,kd->gtk", q_part, k_part, preferred_element_type=jnp.float32)
            * score_scale
        )
        shares = softmax_shares(scores, key_pos[None, None, :] <= query_pos[None, :, None])
        return jnp.einsum("gtk,kd->tgd", shares, v_part, preferred_element_type=jnp.float32).astype(
            jnp.bfloat16
        )

    kv_out = lax.map(one_kv, (query_groups, k_moved, v_moved))
    attended = jnp.moveaxis(kv_out, 0, 1).reshape(token_rows, QUERY_HEADS * HEAD_SIZE)
    node_count = lax.axis_size("node")
    expert_count = EXP_NODE * node_count
    cap_slots = token_rows * TOP * 3 // (2 * expert_count)
    expert_ids = jnp.arange(expert_count, dtype=jnp.int32)
    match = routes[:, :, None] == expert_ids[None, None, :]
    member = jnp.sum(match.astype(jnp.int32), axis=1)
    weight_te = jnp.sum(
        jnp.where(match, gates.astype(jnp.float32)[:, :, None], jnp.float32(0.0)), axis=1
    )
    ranked = jnp.cumsum(member, axis=0) - member
    slot_ids = jnp.arange(cap_slots, dtype=jnp.int32)
    picked = (member[None, :, :] == 1) & (ranked[None, :, :] == slot_ids[:, None, None])
    pick_table = picked.astype(jnp.bfloat16).reshape(cap_slots, token_rows, node_count, EXP_NODE)
    chosen = jnp.einsum("ctnj,tw->jncw", pick_table, attended, preferred_element_type=jnp.float32)
    pick_float = picked.astype(jnp.float32).reshape(cap_slots, token_rows, node_count, EXP_NODE)
    slot_gate = jnp.einsum(
        "ctnj,tnj->jnc",
        pick_float,
        weight_te.reshape(token_rows, node_count, EXP_NODE),
        precision=lax.Precision.HIGHEST,
    )
    outgoing = (chosen * slot_gate[:, :, :, None]).astype(jnp.bfloat16)
    received = lax.all_to_all(outgoing, "node", split_axis=1, concat_axis=1, tiled=True)
    return received[:, None]


def solution(mesh):
    return jax.shard_map(
        per_device,
        mesh=mesh,
        in_specs=(
            P(("node", "seq"), None),
            P(("node", "seq"), None),
            P(("node", "seq"), None),
            P(("node", "seq"), None),
            P(("node", "seq"), None),
        ),
        out_specs=P("node", "seq", None, None, None),
        check_vma=False,
    )
```

profile of v0, /device:TPU:25, one launch (start us, length us, event | category | flops | bytes accessed | tf_op | source)
XLA Modules:
  0.0 228.6 jit_solution(18201360269969400825)
XLA Ops:
  6.5 0.0 copy-start.1
  6.5 0.0 copy-start
  6.5 0.0 all-gather.5.cloned.1.call-start
  6.5 1.9 copy.29
  8.4 0.0 all-gather.5.cloned.1.call-update
  8.4 0.0 all-gather.3.cloned.1.call-start
  8.5 1.8 copy.28
  10.3 0.0 all-gather.3.cloned.1.call-update
  10.3 0.7 convert_element_type.21
  11.0 0.7 convert_reduce_fusion
  11.7 0.2 copy.33
  11.9 0.1 fusion.62
  12.0 0.1 sub.15
  12.1 0.1 copy.35
  12.2 0.0 copy-done.1
  12.2 0.4 fusion.53
  12.6 0.0 copy-done
  12.6 0.7 copy.30
  13.3 46.4 %all-gather.5.cloned.1.call-done = bf16[1024,8,128]{0,2,1:T(8,128)(2,1)} async-done(((bf16[128,8,128]{0,2,1:T(8,128)(2,1)}), bf16[1024,8,128]{0,2,1:T(8,128)(2,1)}) %all-gather.5.cloned.1.call-update) | async-done | bytes 2097168 | tf_op jit(solution)/shard_map/all_gather | solution.py:28
  59.8 51.3 %all-gather.3.cloned.1.call-done = bf16[1024,8,128]{0,2,1:T(8,128)(2,1)} async-done(((bf16[128,8,128]{0,2,1:T(8,128)(2,1)}), bf16[1024,8,128]{0,2,1:T(8,128)(2,1)}) %all-gather.3.cloned.1.call-update) | async-done | bytes 2097168 | tf_op jit(solution)/shard_map/all_gather | solution.py:29
  111.1 32.9 %while.11 = (s32[]{:T(128)}, bf16[8,128,4,128]{1,3,2,0:T(8,128)(2,1)S(1)}, bf16[8,1024,128]{1,2,0:T(8,128)(2,1)}, bf16[8,1024,128]{1,2,0:T(8,128)(2,1)}, bf16[8,...) while((s32[]{:T(128)}, bf16[8,128,4,128]{1,3,2,0:T(8,128)(2,1)S(1)}, ...), condition=%wide.region_3.4_spmd.clone, body=%wide.region_0.3_spmd.clone.sunk | while | flops 407571072 | bytes 1581145 | solution.py:51
  111.1 0.1 iota_compare_fusion.4
  111.2 1.8 fusion.79
  113.0 2.2 fusion.80
  115.2 0.1 iota_compare_fusion.4
  115.3 1.8 fusion.79
  117.1 2.2 fusion.80
  119.4 0.1 iota_compare_fusion.4
  119.5 1.8 fusion.79
  121.3 2.2 fusion.80
  123.5 0.1 iota_compare_fusion.4
  123.6 1.8 fusion.79
  125.4 2.2 fusion.80
  127.6 0.1 iota_compare_fusion.4
  127.7 1.8 fusion.79
  129.5 2.2 fusion.80
  131.7 0.1 iota_compare_fusion.4
  131.8 1.8 fusion.79
  133.6 2.2 fusion.80
  135.8 0.1 iota_compare_fusion.4
  135.9 1.8 fusion.79
  137.8 2.2 fusion.80
  140.0 0.1 iota_compare_fusion.4
  140.1 1.8 fusion.79
  141.9 2.2 fusion.80
  144.1 1.8 fusion.51
  145.9 72.8 %all_to_all.5 = bf16[2,4,96,4096]{3,2,0,1:T(8,128)(2,1)S(1)} all-to-all(bf16[2,4,96,4096]{3,2,0,1:T(8,128)(2,1)S(1)} %fusion.51), channel_id=1, replica_groups=mesh['node'=4,'seq'=8] {'node'}, dimensions={1} | all-to-all | bytes 12582912 | tf_op jit(solution)/shard_map/all_to_all | solution.py:75
  218.6 3.1 %copy.37 = bf16[2,1,4,96,4096]{4,3,2,1,0:T(8,128)(2,1)} copy(bf16[2,1,4,96,4096]{4,3,0,2,1:T(8,128)(2,1)S(1)} %bitcast.95) | data formatting | bytes 12582912 | tf_op jit(solution)/shard_map/broadcast_in_dim | solution.py:76
  (12 shorter events, 0.1 us)
Async XLA Ops:
  6.5 5.6 %copy-start.1 = (s32[128,4]{0,1:T(4,128)S(1)}, s32[128,4]{0,1:T(4,128)}, u32[]{:S(2)}) copy-start(s32[128,4]{0,1:T(4,128)} %param.10) | copy-start | bytes 6148
  6.5 6.1 %copy-start = (bf16[128,4096]{1,0:T(8,128)(2,1)S(1)}, bf16[128,4096]{1,0:T(8,128)(2,1)}, u32[]{:S(2)}) copy-start(bf16[128,4096]{1,0:T(8,128)(2,1)} %param.7) | copy-start | bytes 3145732
  6.5 53.2 %all-gather.5.cloned.1.call-start = ((), (), s32[]{:S(2)}) async-start(), calls=%async_computation.2 | async-start | bytes 2359296 | tf_op jit(solution)/shard_map/all_gather | solution.py:28
  8.4 102.7 %all-gather.3.cloned.1.call-start = ((), (), s32[]{:S(2)}) async-start(), calls=%async_computation.1 | async-start | bytes 2359296 | tf_op jit(solution)/shard_map/all_gather | solution.py:29
Sparse Core Ops, SparseCore 0:
  9.4 50.3 all-gather.4
  61.8 49.2 all-gather.2
where the time goes:
time: 233 us; the launch traced here: 229 us
  waiting for transfers between devices  97.8 us (42%)
  blocking collectives  72.8 us (31%)
  matrix products  34.1 us (15%)
  between operations  13.5 us (6%)
  local copies, waits for them, and re-layouts  7.74 us (3%)
  other arithmetic  2.37 us (1%)
    all_to_all x1, blocking collectives, per_device(): lax.all_to_all(outgoing, 'node', split_axis=1, concat_axis=1, tiled=True)  72.8 us
    all_gather x1, waiting for transfers between devices, per_device(): lax.all_gather(value_triple, 'seq', axis=0, tiled=True)  51.3 us
    all_gather x1, waiting for transfers between devices, per_device(): lax.all_gather(key_triple, 'seq', axis=0, tiled=True)  46.4 us
    dot_general x8, matrix products, one_kv(): jnp.einsum('gtk,kd->tgd', shares, v_part, preferred_element_type=jnp.floa...  17.4 us
    sub x8, matrix products, softmax_shares(): raised = jnp.exp(scores - top_score)  14.5 us
  transfers between devices with their start and end apart: 2, of which 2 were waited for; matrix products, arithmetic and copies ran while one was open for 2% of the time, Pallas kernels for 0%

commit v1 on v0

v1 whole, which is shorter than its diff:
```python
import functools

import jax
import jax.numpy as jnp
from jax import lax
from jax.experimental import pallas as pl
from jax.experimental.pallas import tpu as pltpu
from jax.sharding import PartitionSpec as P

QUERY_HEADS = 32
KEY_VALUE_HEADS = 8
HEAD_SIZE = 128
TOP = 4
EXP_NODE = 2
MEMBERS = QUERY_HEADS // KEY_VALUE_HEADS
GROUP_COLS = MEMBERS * HEAD_SIZE
LOG2E = 1.4426950408889634
MESH = pl.DeviceIdType.MESH


def attend_kernel(
    n_node, n_seq, rows,
    q_ref, wt_ref, k_hbm, v_hbm, all_hbm, wts_hbm,
    kv, att, kv_local, kv_recv, z_send, x_send,
    a_local, a_recv, a_core, a_far, a_fwd, w_local, w_recv, w_send,
):
    n = lax.axis_index("node")
    s = lax.axis_index("seq")
    a, b = s // 2, lax.rem(s, 2)
    depth = n_seq // 2
    far = n_node // 2
    y, core = n // 2, lax.rem(n, 2)
    mate = 2 * y + 1 - core
    beside = 2 * a + 1 - b
    groups = KEY_VALUE_HEADS

    def remote(src, dst, send, recv, node, seq):
        return pltpu.make_async_remote_copy(
            src_ref=src, dst_ref=dst, send_sem=send, recv_sem=recv,
            device_id=(node, seq), device_id_type=MESH,
        )

    def own_copy(c, which):
        src = (k_hbm, v_hbm)[which].at[:, pl.ds(pl.multiple_of(c * HEAD_SIZE, HEAD_SIZE), HEAD_SIZE)]
        dst = kv.at[c, which, pl.ds(pl.multiple_of(s * rows, rows), rows), :]
        return pltpu.make_async_copy(src, dst, kv_local.at[c, which])

    def block(c, j):
        return kv.at[c, :, pl.ds(pl.multiple_of(j * rows, rows), rows), :]

    def z_copy(c, line):
        ref = block(c, 2 * line + b)
        return remote(ref, ref, z_send.at[c, line], kv_recv.at[c, 2 * line + b], n, s + 2)

    def x_copy(c, line):
        ref = block(c, 2 * line + b)
        return remote(ref, ref, x_send.at[c, line], kv_recv.at[c, 2 * line + b], n, beside)

    def kv_arrived(c, j):
        ref = block(c, j)
        remote(ref, ref, z_send.at[c, 0], kv_recv.at[c, j], n, beside).wait_recv()

    def loop(body):
        def step(c, carry):
            body(c)
            return carry
        lax.fori_loop(0, groups, step, 0)

    def load(c):
        own_copy(c, 0).start()
        own_copy(c, 1).start()

    loop(load)

    barrier = pltpu.get_barrier_semaphore()

    def greet(node, seq):
        pl.semaphore_signal(barrier, inc=1, device_id=(node, seq), device_id_type=MESH)

    greet(n, beside)
    for k in range(1, n_node):
        greet(lax.rem(n + k, n_node), s)

    @pl.when(a > 0)
    def _():
        greet(n, s - 2)

    @pl.when(a < depth - 1)
    def _():
        greet(n, s + 2)

    edges = (a > 0).astype(jnp.int32) + (a < depth - 1).astype(jnp.int32)
    pl.semaphore_wait(barrier, n_node + edges)

    def pass_on(c, line, own):
        @pl.when(a < depth - 1)
        def _():
            z_copy(c, line).start()

        if own:
            @pl.when(b == 0)
            def _():
                x_copy(c, line).start()
        else:
            x_copy(c, line).start()

    def own_out(c):
        own_copy(c, 0).wait()
        own_copy(c, 1).wait()
        pass_on(c, a, True)

    def forward(c):
        for lag in range(1, depth):
            @pl.when(lag <= a)
            def _():
                line = a - lag
                kv_arrived(c, 2 * line + b)
                pass_on(c, line, False)

    def x_arrivals(c):
        @pl.when(b == 1)
        def _():
            kv_arrived(c, 2 * a)

        for lag in range(1, depth):
            @pl.when(lag <= a)
            def _():
                kv_arrived(c, 2 * (a - lag) + 1 - b)

    def wide(c):
        return pl.ds(pl.multiple_of(c * GROUP_COLS, GROUP_COLS), GROUP_COLS)

    def landing(c, node):
        return all_hbm.at[node, :, wide(c)]

    def att_local(c):
        return pltpu.make_async_copy(att.at[:, wide(c)], landing(c, n), a_local.at[c])

    def att_core(c):
        return remote(att.at[:, wide(c)], landing(c, n), a_core.at[c], a_recv.at[c, n], mate, s)

    def att_far(c, k):
        other = 2 * lax.rem(y + k, far) + core
        return remote(att.at[:, wide(c)], landing(c, n), a_far.at[c, k], a_recv.at[c, n], other, s)

    def att_fwd(c, k):
        origin = 2 * lax.rem(y + k, far) + core
        ref = landing(c, origin)
        return remote(ref, ref, a_fwd.at[c, k], a_recv.at[c, origin], mate, s)

    def att_arrived(c, node):
        ref = landing(c, node)
        remote(ref, ref, a_core.at[c], a_recv.at[c, node], mate, s).wait_recv()

    def att_forward(c):
        for k in range(1, far):
            att_arrived(c, 2 * lax.rem(y + k, far) + core)
            att_fwd(c, k).start()

    span = n_seq * rows
    query_pos = s * rows + lax.broadcasted_iota(jnp.int32, (rows, span), 0)
    allowed = lax.broadcasted_iota(jnp.int32, (rows, span), 1) <= query_pos

    def compute(c):
        k_part = kv[c, 0]
        v_part = kv[c, 1]
        for h in range(MEMBERS):
            cols = pl.ds(pl.multiple_of(c * GROUP_COLS + h * HEAD_SIZE, HEAD_SIZE), HEAD_SIZE)
            scores = lax.dot_general(
                q_ref[:, cols], k_part, (((1,), (1,)), ((), ())),
                preferred_element_type=jnp.float32,
            )
            scores = jnp.where(allowed, scores, jnp.float32(-1e30))
            top = jnp.max(scores, axis=1, keepdims=True)
            raised = jnp.exp2((scores - top) * jnp.float32(HEAD_SIZE ** -0.5 * LOG2E))
            total = jnp.sum(raised, axis=1, keepdims=True)
            shares = (raised * (1.0 / total)).astype(jnp.bfloat16)
            att[:, cols] = jnp.dot(
                shares, v_part, preferred_element_type=jnp.float32
            ).astype(jnp.bfloat16)

    def send_att(c):
        for k in range(1, far):
            att_far(c, k).start()
        att_core(c).start()
        att_local(c).start()

    def w_copy(k):
        other = lax.rem(n + k, n_node)
        return remote(wt_ref, wts_hbm.at[n], w_send.at[k], w_recv.at[n], other, s)

    own_out(0)
    own_out(1)

    pltpu.make_async_copy(wt_ref, wts_hbm.at[n], w_local).start()
    for k in range(1, n_node):
        w_copy(k).start()

    def clear(j, carry):
        kv[:, :, pl.ds(pl.multiple_of(j * rows, rows), rows), :] = jnp.zeros(
            (groups, 2, rows, HEAD_SIZE), jnp.bfloat16
        )
        return carry

    lax.fori_loop(s + 1, n_seq, clear, 0)

    forward(0)

    def step(c):
        @pl.when(c + 2 < groups)
        def _():
            own_out(c + 2)

        @pl.when(c + 1 < groups)
        def _():
            forward(c + 1)

        x_arrivals(c)
        compute(c)
        send_att(c)

        @pl.when(c > 0)
        def _():
            att_forward(c - 1)

    loop(step)
    att_forward(groups - 1)

    def drain(c):
        @pl.when(a < depth - 1)
        def _():
            z_copy(c, a).wait_send()

        @pl.when(b == 0)
        def _():
            x_copy(c, a).wait_send()

        for lag in range(1, depth):
            @pl.when(lag <= a)
            def _():
                x_copy(c, a - lag).wait_send()

                @pl.when(a < depth - 1)
                def _():
                    z_copy(c, a - lag).wait_send()

        att_local(c).wait()
        att_core(c).wait_send()
        att_arrived(c, mate)
        for k in range(1, far):
            att_far(c, k).wait_send()
            att_fwd(c, k).wait_send()
            att_arrived(c, 2 * lax.rem(y + k, far) + 1 - core)

    loop(drain)
    pltpu.make_async_copy(wt_ref, wts_hbm.at[n], w_local).wait()
    for k in range(1, n_node):
        w_copy(k).wait_send()
        origin = lax.rem(n + k, n_node)
        remote(wt_ref, wts_hbm.at[origin], w_send.at[k], w_recv.at[origin], mate, s).wait_recv()


def attend(n_node, n_seq, q, wt, k, v):
    rows = q.shape[0]
    groups, far = KEY_VALUE_HEADS, n_node // 2
    dma = pltpu.SemaphoreType.DMA
    return pl.pallas_call(
        functools.partial(attend_kernel, n_node, n_seq, rows),
        out_shape=(
            jax.ShapeDtypeStruct((n_node,) + q.shape, jnp.bfloat16),
            jax.ShapeDtypeStruct((n_node,) + wt.shape, jnp.float32),
        ),
        in_specs=[
            pl.BlockSpec(memory_space=pltpu.VMEM),
            pl.BlockSpec(memory_space=pltpu.VMEM),
            pl.BlockSpec(memory_space=pl.ANY),
            pl.BlockSpec(memory_space=pl.ANY),
        ],
        out_specs=(pl.BlockSpec(memory_space=pl.ANY), pl.BlockSpec(memory_space=pl.ANY)),
        scratch_shapes=[
            pltpu.VMEM((groups, 2, n_seq * rows, HEAD_SIZE), jnp.bfloat16),
            pltpu.VMEM(q.shape, jnp.bfloat16),
            dma((groups, 2)),
            dma((groups, n_seq)),
            dma((groups, n_seq // 2)),
            dma((groups, n_seq // 2)),
            dma((groups,)),
            dma((groups, n_node)),
            dma((groups,)),
            dma((groups, far)),
            dma((groups, far)),
            dma,
            dma((n_node,)),
            dma((n_node,)),
        ],
        compiler_params=pltpu.CompilerParams(
            collective_id=0, has_side_effects=True, vmem_limit_bytes=48 * 1024 * 1024
        ),
    )(q, wt, k, v)


def pick_kernel(cap, att_ref, wt_ref, out_ref):
    rows, width = att_ref.shape[1:]
    first = EXP_NODE * lax.axis_index("node")
    earlier = lax.broadcasted_iota(jnp.int32, (rows, rows), 0) < lax.broadcasted_iota(
        jnp.int32, (rows, rows), 1
    )
    earlier = earlier.astype(jnp.float32).astype(jnp.bfloat16)
    slots = lax.broadcasted_iota(jnp.int32, (cap, rows), 0).astype(jnp.float32)
    for e in range(EXP_NODE):
        weight = jnp.broadcast_to(wt_ref[0, pl.ds(first + e, 1), :], (8, rows))
        member = jnp.where(weight > 0, jnp.float32(1.0), jnp.float32(0.0))
        rank = jnp.dot(member.astype(jnp.bfloat16), earlier, preferred_element_type=jnp.float32)
        gate = jnp.broadcast_to(weight[:1], (cap, rows))
        place = jnp.broadcast_to(rank[:1], (cap, rows))
        table = jnp.where((gate > 0) & (place == slots), gate, 0.0).astype(jnp.bfloat16)
        for at in range(0, width, 1024):
            out_ref[e, 0, 0, :, at : at + 1024] = jnp.dot(
                table, att_ref[0, :, at : at + 1024], preferred_element_type=jnp.float32
            ).astype(jnp.bfloat16)


def pick(cap, att, wts):
    n_node, rows, width = att.shape
    return pl.pallas_call(
        functools.partial(pick_kernel, cap),
        grid=(n_node,),
        out_shape=jax.ShapeDtypeStruct((EXP_NODE, 1, n_node, cap, width), jnp.bfloat16),
        in_specs=[
            pl.BlockSpec((1, rows, width), lambda i: (i, 0, 0)),
            pl.BlockSpec((1,) + wts.shape[1:], lambda i: (i, 0, 0)),
        ],
        out_specs=pl.BlockSpec((EXP_NODE, 1, 1, cap, width), lambda i: (0, 0, i, 0, 0)),
        compiler_params=pltpu.CompilerParams(vmem_limit_bytes=32 * 1024 * 1024),
    )(att, wts)


def per_device(n_node, n_seq, queries, keys, values, routes, gates):
    experts = EXP_NODE * n_node
    cap = queries.shape[0] * TOP * 3 // (2 * experts)
    match = routes[None, :, :] == jnp.arange(experts, dtype=jnp.int32)[:, None, None]
    wt = jnp.sum(jnp.where(match, gates.astype(jnp.float32)[None], jnp.float32(0.0)), axis=2)
    att, wts = attend(n_node, n_seq, queries, wt, keys, values)
    return pick(cap, att, wts)


def solution(mesh):
    spec = P(("node", "seq"), None)
    return jax.shard_map(
        functools.partial(per_device, mesh.shape["node"], mesh.shape["seq"]),
        mesh=mesh,
        in_specs=(spec,) * 5,
        out_specs=P("node", "seq", None, None, None),
        check_vma=False,
    )
```

time: 233 us -> 69.5 us (0.30); the launches traced: 229 us -> 68.4 us
  waiting for transfers between devices: 97.8 us -> 0 us
  blocking collectives: 72.8 us -> 0 us
  Pallas kernels: 0 us -> 63.9 us
  matrix products: 34.1 us -> 0 us
  between operations: 13.5 us -> 0.01 us
  local copies, waits for them, and re-layouts: 7.74 us -> 3.12 us
    all_gather x2 -> x0, waiting for transfers between devices: 97.8 us -> none  [the longest x1 51.3 us: per_device(): lax.all_gather(value_triple, 'seq', axis=0, tiled=True)]
    all_to_all x1 -> x0, blocking collectives: 72.8 us -> none  [per_device(): lax.all_to_all(outgoing, 'node', split_axis=1, concat_axis=1, tiled=True)]
    pallas_call x0 -> x2, Pallas kernels: none -> 63.9 us  [the longest x1 59.1 us: attend(): pl.pallas_call(functools.partial(attend_kernel, n_node, n_seq, rows), out...]
    dot_general x10 -> x0, matrix products: 19.6 us -> none  [the longest x8 17.4 us: one_kv(): jnp.einsum('gtk,kd->tgd', shares, v_part, preferred_element_type=jnp.floa...]
    sub x8 -> x0, matrix products: 14.5 us -> none  [softmax_shares(): raised = jnp.exp(scores - top_score)]
    broadcast_in_dim x1 -> x0, local copies, waits for them, and re-layouts: 3.13 us -> none  [per_device(): return received[:, None]]
  transfers between devices with their start and end apart: 2 -> 0, of which waited for: 2 -> 0; matrix products, arithmetic and copies ran while one was open for 2% -> 0% of each run, Pallas kernels for 0% -> 0%
where the time goes in v1:
time: 69.5 us; the launch traced here: 68.4 us
  Pallas kernels  63.9 us (92%)
  local copies, waits for them, and re-layouts  3.12 us (4%)
  other arithmetic  1.37 us (2%)
    pallas_call x1, Pallas kernels, attend(): pl.pallas_call(functools.partial(attend_kernel, n_node, n_seq, rows), out...  59.1 us
    pallas_call x1, Pallas kernels, pick(): pl.pallas_call(functools.partial(pick_kernel, cap), grid=(n_node,), out_s...  4.83 us
    unnamed x6, local copies, waits for them, and re-layouts  3.12 us

profile of v1, /device:TPU:25, one launch (start us, length us, event | category | flops | bytes accessed | tf_op | source)
XLA Modules:
  0.0 68.4 jit_solution(12809740086153134560)
XLA Ops:
  0.0 0.7 convert_element_type.3
  0.7 0.7 %select_reduce_fusion.wt_ref = f32[8,128]{1,0:T(8,128)S(1)} fusion(f32[128,4]{0,1:T(4,128)S(1)} %convert_element_type.3, s32[128,4]{0,1:T(4,128)} %param.8), kind=kLoop, calls=%fused_computation | loop fusion | flops 11264 | bytes 8192 | tf_op jit(solution)/shard_map/reduce_sum | solution.py:342
  1.4 0.0 copy-start
  1.4 1.2 %copy-done = bf16[128,4096]{1,0:T(8,128)(2,1)S(1)} copy-done((bf16[128,4096]{1,0:T(8,128)(2,1)S(1)}, bf16[128,4096]{1,0:T(8,128)(2,1)}, u32[]{:S(2)}) %copy-start) | copy-done | bytes 1048600
  2.6 0.0 copy-start.1
  2.6 0.9 %copy-done.1 = bf16[128,1024]{1,0:T(8,128)(2,1)S(1)} copy-done((bf16[128,1024]{1,0:T(8,128)(2,1)S(1)}, bf16[128,1024]{1,0:T(8,128)(2,1)}, u32[]{:S(2)}) %copy-start.1) | copy-done | bytes 262168
  3.5 0.0 copy-start.2
  3.5 0.9 %copy-done.2 = bf16[128,1024]{1,0:T(8,128)(2,1)S(1)} copy-done((bf16[128,1024]{1,0:T(8,128)(2,1)S(1)}, bf16[128,1024]{1,0:T(8,128)(2,1)}, u32[]{:S(2)}) %copy-start.2) | copy-done | bytes 262168
  4.5 59.1 %shard_map.55 = (bf16[4,128,4096]{2,1,0:T(8,128)(2,1)S(1)}, f32[4,8,128]{2,1,0:T(8,128)S(1)}) custom-call(bf16[128,4096]{1,0:T(8,128)(2,1)S(1)} %copy-done, f32[8,128]{1,0:T(8,128)S(1)} %select_reduce_fusion.wt_ref, bf16[128,1024]{1,0:T(8,128)(2,1)S(1)} %copy-done.1, bf16[128,1024]{1,0:T(8,128)(2,1)S(1)} %copy-done.2), custom_call_target="tpu_custom_call" | custom-call | tf_op jit(solution)/shard_map/pallas_call | solution.py:267
  63.6 4.8 %shard_map.56 = bf16[2,1,4,96,4096]{4,3,2,1,0:T(8,128)(2,1)} custom-call(bf16[4,128,4096]{2,1,0:T(8,128)(2,1)S(1)} %get-tuple-element.7.att_ref, f32[4,8,128]{2,1,0:T(8,128)S(1)} %get-tuple-element.8.wt_ref), custom_call_target="tpu_custom_call" | custom-call | tf_op jit(solution)/shard_map/pallas_call | solution.py:325
Async XLA Ops:
  1.4 1.2 %copy-start = (bf16[128,4096]{1,0:T(8,128)(2,1)S(1)}, bf16[128,4096]{1,0:T(8,128)(2,1)}, u32[]{:S(2)}) copy-start(bf16[128,4096]{1,0:T(8,128)(2,1)} %q_ref.1) | copy-start | bytes 3145732
  2.6 0.9 %copy-start.1 = (bf16[128,1024]{1,0:T(8,128)(2,1)S(1)}, bf16[128,1024]{1,0:T(8,128)(2,1)}, u32[]{:S(2)}) copy-start(bf16[128,1024]{1,0:T(8,128)(2,1)} %k_hbm.1) | copy-start | bytes 786436
  3.5 0.9 %copy-start.2 = (bf16[128,1024]{1,0:T(8,128)(2,1)S(1)}, bf16[128,1024]{1,0:T(8,128)(2,1)}, u32[]{:S(2)}) copy-start(bf16[128,1024]{1,0:T(8,128)(2,1)} %v_hbm.1) | copy-start | bytes 786436

commit v2 on v1

v2 whole, which is shorter than its diff:
```python
import functools

import jax
import jax.numpy as jnp
from jax import lax
from jax.experimental import pallas as pl
from jax.experimental.pallas import tpu as pltpu
from jax.sharding import PartitionSpec as P

QUERY_HEADS = 32
KEY_VALUE_HEADS = 8
HEAD_SIZE = 128
TOP = 4
EXP_NODE = 2
MEMBERS = QUERY_HEADS // KEY_VALUE_HEADS
GROUP_COLS = MEMBERS * HEAD_SIZE
LOG2E = 1.4426950408889634
MESH = pl.DeviceIdType.MESH


def attend_kernel(
    n_node, n_seq, rows,
    wt_ref, q_hbm, k_hbm, v_hbm, all_hbm, wts_hbm,
    kv, qs, att, kv_local, kv_send, kv_recv, q_local, q_send, q_recv, z_send, z_recv,
    x_send, x_recv, a_local, a_recv, a_core, a_far, a_fwd, w_local, w_recv, w_send,
):
    n = lax.axis_index("node")
    s = lax.axis_index("seq")
    a, b = s // 2, lax.rem(s, 2)
    depth = n_seq // 2
    far = n_node // 2
    y, core = n // 2, lax.rem(n, 2)
    mate = 2 * y + 1 - core
    beside = 2 * a + 1 - b
    steps = KEY_VALUE_HEADS // 2

    def remote(src, dst, send, recv, node, seq):
        return pltpu.make_async_remote_copy(
            src_ref=src, dst_ref=dst, send_sem=send, recv_sem=recv,
            device_id=(node, seq), device_id_type=MESH,
        )

    def span_of(index, size):
        return pl.ds(pl.multiple_of(index * size, size), size)

    def kv_source(half, c, which):
        return (k_hbm, v_hbm)[which].at[:, span_of(half * steps + c, HEAD_SIZE)]

    def kv_rows(c, which, j):
        return kv.at[c, which, span_of(j, rows), :]

    def kv_keep(c, which):
        return pltpu.make_async_copy(
            kv_source(b, c, which), kv_rows(c, which, s), kv_local.at[c, which]
        )

    def kv_give(c, which):
        return remote(
            kv_source(1 - b, c, which), kv_rows(c, which, s),
            kv_send.at[c, which], kv_recv.at[c, which], n, beside,
        )

    def kv_taken(c, which):
        ref = kv_rows(c, which, beside)
        return remote(ref, ref, kv_send.at[c, which], kv_recv.at[c, which], n, beside)

    def q_source(half, c):
        return q_hbm.at[:, span_of(half * steps + c, GROUP_COLS)]

    def q_keep(c):
        return pltpu.make_async_copy(q_source(b, c), qs.at[c, b], q_local.at[c])

    def q_give(c):
        return remote(
            q_source(1 - b, c), qs.at[c, b], q_send.at[c], q_recv.at[c], n, beside
        )

    def q_taken(c):
        ref = qs.at[c, 1 - b]
        return remote(ref, ref, q_send.at[c], q_recv.at[c], n, beside)

    def z_copy(c, line):
        ref = kv.at[c, :, span_of(line, 2 * rows), :]
        return remote(ref, ref, z_send.at[c, line], z_recv.at[c, line], n, s + 2)

    def z_arrived(c, line):
        ref = kv.at[c, :, span_of(line, 2 * rows), :]
        remote(ref, ref, z_send.at[c, line], z_recv.at[c, line], n, beside).wait_recv()

    def loop(body):
        def step(c, carry):
            body(c)
            return carry
        lax.fori_loop(0, steps, step, 0)

    def load(c):
        kv_keep(c, 0).start()
        kv_keep(c, 1).start()
        q_keep(c).start()

    loop(load)

    barrier = pltpu.get_barrier_semaphore()

    def greet(node, seq):
        pl.semaphore_signal(barrier, inc=1, device_id=(node, seq), device_id_type=MESH)

    greet(n, beside)
    for k in range(1, n_node):
        greet(lax.rem(n + k, n_node), s)

    @pl.when(a > 0)
    def _():
        greet(n, s - 2)

    @pl.when(a < depth - 1)
    def _():
        greet(n, s + 2)

    edges = (a > 0).astype(jnp.int32) + (a < depth - 1).astype(jnp.int32)
    pl.semaphore_wait(barrier, n_node + edges)

    def give_kv(c):
        kv_give(c, 0).start()
        kv_give(c, 1).start()

    loop(give_kv)
    loop(lambda c: q_give(c).start())

    def pair_out(c):
        for which in range(2):
            kv_keep(c, which).wait()
            kv_taken(c, which).wait_recv()

        @pl.when(a < depth - 1)
        def _():
            z_copy(c, a).start()

    def forward(c, send):
        for lag in range(1, depth):
            @pl.when(lag <= a)
            def _():
                z_arrived(c, a - lag)
                if send:
                    z_copy(c, a - lag).start()

    def landing(half, c, node):
        return all_hbm.at[node, :, span_of(half * steps + c, GROUP_COLS)]

    def x_give(c):
        return remote(att.at[c, 1 - b], landing(b, c, n), x_send.at[c], x_recv.at[c], n, beside)

    def x_taken(c):
        ref = landing(1 - b, c, n)
        return remote(ref, ref, x_send.at[c], x_recv.at[c], n, beside)

    def att_local(c):
        return pltpu.make_async_copy(att.at[c, b], landing(b, c, n), a_local.at[c])

    def att_from(own, half, c):
        return att.at[c, b] if own else landing(half, c, n)

    def att_core(own, half, c):
        return remote(
            att_from(own, half, c), landing(half, c, n),
            a_core.at[half, c], a_recv.at[half, c, n], mate, s,
        )

    def att_far(own, half, c, k):
        other = 2 * lax.rem(y + k, far) + core
        return remote(
            att_from(own, half, c), landing(half, c, n),
            a_far.at[half, c, k], a_recv.at[half, c, n], other, s,
        )

    def att_fwd(half, c, k):
        origin = 2 * lax.rem(y + k, far) + core
        ref = landing(half, c, origin)
        return remote(ref, ref, a_fwd.at[half, c, k], a_recv.at[half, c, origin], mate, s)

    def att_arrived(half, c, node):
        ref = landing(half, c, node)
        remote(ref, ref, a_core.at[half, c], a_recv.at[half, c, node], mate, s).wait_recv()

    def att_forward(half, c):
        for k in range(1, far):
            att_arrived(half, c, 2 * lax.rem(y + k, far) + core)
            att_fwd(half, c, k).start()

    def spread(own, half, c):
        for k in range(1, far):
            att_far(own, half, c, k).start()
        att_core(own, half, c).start()

    def relay(c):
        x_taken(c).wait_recv()
        spread(False, 1 - b, c)

    span = n_seq * rows
    key_pos = lax.broadcasted_iota(jnp.int32, (rows, span), 1)
    row_at = lax.broadcasted_iota(jnp.int32, (rows, span), 0)

    def compute(c, p):
        allowed = key_pos - row_at <= (2 * a + p) * rows
        allowed = jnp.concatenate([allowed] * MEMBERS, axis=0)
        q_part = qs[c, p]
        stacked = jnp.concatenate(
            [q_part[:, h * HEAD_SIZE : (h + 1) * HEAD_SIZE] for h in range(MEMBERS)], axis=0
        )
        scores = lax.dot_general(
            stacked, kv[c, 0], (((1,), (1,)), ((), ())), preferred_element_type=jnp.float32
        )
        scores = jnp.where(allowed, scores, jnp.float32(-1e30))
        top = jnp.max(scores, axis=1, keepdims=True)
        raised = jnp.exp2((scores - top) * jnp.float32(HEAD_SIZE ** -0.5 * LOG2E))
        total = jnp.sum(raised, axis=1, keepdims=True)
        shares = (raised * (1.0 / total)).astype(jnp.bfloat16)
        result = jnp.dot(shares, kv[c, 1], preferred_element_type=jnp.float32).astype(jnp.bfloat16)
        for h in range(MEMBERS):
            att[c, p, :, h * HEAD_SIZE : (h + 1) * HEAD_SIZE] = result[h * rows : (h + 1) * rows]

    def w_copy(k):
        other = lax.rem(n + k, n_node)
        return remote(wt_ref, wts_hbm.at[n], w_send.at[k], w_recv.at[n], other, s)

    def clear(j, carry):
        kv[:, :, span_of(j, rows), :] = jnp.zeros((steps, 2, rows, HEAD_SIZE), jnp.bfloat16)
        return carry

    lax.fori_loop(2 * a + 2, n_seq, clear, 0)
    pair_out(0)
    pair_out(1)

    pltpu.make_async_copy(wt_ref, wts_hbm.at[n], w_local).start()
    for k in range(1, n_node):
        w_copy(k).start()

    @pl.when(a < depth - 1)
    def _():
        forward(0, True)

    def step(c):
        @pl.when(c + 2 < steps)
        def _():
            pair_out(c + 2)

        @pl.when((a < depth - 1) & (c + 1 < steps))
        def _():
            forward(c + 1, True)

        @pl.when(a == depth - 1)
        def _():
            forward(c, False)

        q_taken(c).wait_recv()
        compute(c, 1 - b)
        x_give(c).start()

        @pl.when(c > 0)
        def _():
            relay(c - 1)

        q_keep(c).wait()
        compute(c, b)
        att_local(c).start()
        spread(True, b, c)

        @pl.when(c > 0)
        def _():
            att_forward(b, c - 1)
            att_forward(1 - b, c - 1)

    loop(step)
    relay(steps - 1)
    att_forward(b, steps - 1)
    att_forward(1 - b, steps - 1)

    def drain(c):
        for which in range(2):
            kv_give(c, which).wait_send()
        q_give(c).wait_send()
        x_give(c).wait_send()

        @pl.when(a < depth - 1)
        def _():
            for lag in range(depth):
                @pl.when(lag <= a)
                def _():
                    z_copy(c, a - lag).wait_send()

        att_local(c).wait()
        for own in (True, False):
            half = b if own else 1 - b
            att_core(own, half, c).wait_send()
            att_arrived(half, c, mate)
            for k in range(1, far):
                att_far(own, half, c, k).wait_send()
                att_fwd(half, c, k).wait_send()
                att_arrived(half, c, 2 * lax.rem(y + k, far) + 1 - core)

    loop(drain)
    pltpu.make_async_copy(wt_ref, wts_hbm.at[n], w_local).wait()
    for k in range(1, n_node):
        w_copy(k).wait_send()
        origin = lax.rem(n + k, n_node)
        remote(wt_ref, wts_hbm.at[origin], w_send.at[k], w_recv.at[origin], mate, s).wait_recv()


def attend(n_node, n_seq, q, wt, k, v):
    rows = q.shape[0]
    steps, far, depth = KEY_VALUE_HEADS // 2, n_node // 2, n_seq // 2
    dma = pltpu.SemaphoreType.DMA
    hbm = pl.BlockSpec(memory_space=pl.ANY)
    return pl.pallas_call(
        functools.partial(attend_kernel, n_node, n_seq, rows),
        out_shape=(
            jax.ShapeDtypeStruct((n_node,) + q.shape, jnp.bfloat16),
            jax.ShapeDtypeStruct((n_node,) + wt.shape, jnp.float32),
        ),
        in_specs=[pl.BlockSpec(memory_space=pltpu.VMEM), hbm, hbm, hbm],
        out_specs=(hbm, hbm),
        scratch_shapes=[
            pltpu.VMEM((steps, 2, n_seq * rows, HEAD_SIZE), jnp.bfloat16),
            pltpu.VMEM((steps, 2, rows, GROUP_COLS), jnp.bfloat16),
            pltpu.VMEM((steps, 2, rows, GROUP_COLS), jnp.bfloat16),
            dma((steps, 2)), dma((steps, 2)), dma((steps, 2)),
            dma((steps,)), dma((steps,)), dma((steps,)),
            dma((steps, depth)), dma((steps, depth)),
            dma((steps,)), dma((steps,)),
            dma((steps,)),
            dma((2, steps, n_node)),
            dma((2, steps)),
            dma((2, steps, far)),
            dma((2, steps, far)),
            dma,
            dma((n_node,)),
            dma((n_node,)),
        ],
        compiler_params=pltpu.CompilerParams(
            collective_id=0, has_side_effects=True, vmem_limit_bytes=60 * 1024 * 1024
        ),
    )(wt, q, k, v)


def pick_kernel(cap, att_ref, wt_ref, out_ref):
    rows, width = att_ref.shape[1:]
    first = EXP_NODE * lax.axis_index("node")
    earlier = lax.broadcasted_iota(jnp.int32, (rows, rows), 0) < lax.broadcasted_iota(
        jnp.int32, (rows, rows), 1
    )
    earlier = earlier.astype(jnp.float32).astype(jnp.bfloat16)
    slots = lax.broadcasted_iota(jnp.int32, (cap, rows), 0).astype(jnp.float32)
    for e in range(EXP_NODE):
        weight = jnp.broadcast_to(wt_ref[0, pl.ds(first + e, 1), :], (8, rows))
        member = jnp.where(weight > 0, jnp.float32(1.0), jnp.float32(0.0))
        rank = jnp.dot(member.astype(jnp.bfloat16), earlier, preferred_element_type=jnp.float32)
        gate = jnp.broadcast_to(weight[:1], (cap, rows))
        place = jnp.broadcast_to(rank[:1], (cap, rows))
        table = jnp.where((gate > 0) & (place == slots), gate, 0.0).astype(jnp.bfloat16)
        for at in range(0, width, 1024):
            out_ref[e, 0, 0, :, at : at + 1024] = jnp.dot(
                table, att_ref[0, :, at : at + 1024], preferred_element_type=jnp.float32
            ).astype(jnp.bfloat16)


def pick(cap, att, wts):
    n_node, rows, width = att.shape
    return pl.pallas_call(
        functools.partial(pick_kernel, cap),
        grid=(n_node,),
        out_shape=jax.ShapeDtypeStruct((EXP_NODE, 1, n_node, cap, width), jnp.bfloat16),
        in_specs=[
            pl.BlockSpec((1, rows, width), lambda i: (i, 0, 0)),
            pl.BlockSpec((1,) + wts.shape[1:], lambda i: (i, 0, 0)),
        ],
        out_specs=pl.BlockSpec((EXP_NODE, 1, 1, cap, width), lambda i: (0, 0, i, 0, 0)),
        compiler_params=pltpu.CompilerParams(vmem_limit_bytes=60 * 1024 * 1024),
    )(att, wts)


def per_device(n_node, n_seq, queries, keys, values, routes, gates):
    experts = EXP_NODE * n_node
    cap = queries.shape[0] * TOP * 3 // (2 * experts)
    match = routes[None, :, :] == jnp.arange(experts, dtype=jnp.int32)[:, None, None]
    wt = jnp.sum(jnp.where(match, gates.astype(jnp.float32)[None], jnp.float32(0.0)), axis=2)
    att, wts = attend(n_node, n_seq, queries, wt, keys, values)
    return pick(cap, att, wts)


def solution(mesh):
    spec = P(("node", "seq"), None)
    return jax.shard_map(
        functools.partial(per_device, mesh.shape["node"], mesh.shape["seq"]),
        mesh=mesh,
        in_specs=(spec,) * 5,
        out_specs=P("node", "seq", None, None, None),
        check_vma=False,
    )
```

time: 69.5 us -> 67 us (0.964); the launches traced: 68.4 us -> 66.8 us
  local copies, waits for them, and re-layouts: 3.12 us -> 0 us
  Pallas kernels: 63.9 us -> 64.8 us
    unnamed x6 -> x0, local copies, waits for them, and re-layouts: 3.12 us -> none
    pallas_call x1, Pallas kernels: 4.83 us -> 6.8 us  [pick(): pl.pallas_call(functools.partial(pick_kernel, cap), grid=(n_node,), out_s...]
    pallas_call x1, Pallas kernels: 59.1 us -> 58 us  [attend(): pl.pallas_call(functools.partial(attend_kernel, n_node, n_seq, rows), out...]
where the time goes in v2:
time: 67 us; the launch traced here: 66.8 us
  Pallas kernels  64.8 us (97%)
  other arithmetic  1.96 us (3%)
    pallas_call x1, Pallas kernels, attend(): pl.pallas_call(functools.partial(attend_kernel, n_node, n_seq, rows), out...  58 us
    pallas_call x1, Pallas kernels, pick(): pl.pallas_call(functools.partial(pick_kernel, cap), grid=(n_node,), out_s...  6.8 us

profile of v2, /device:TPU:25, one launch (start us, length us, event | category | flops | bytes accessed | tf_op | source)
XLA Modules:
  0.0 66.8 jit_solution(5676362771401242686)
XLA Ops:
  0.0 0.7 %convert_element_type.3 = f32[128,4]{0,1:T(4,128)S(1)} convert(bf16[128,4]{0,1:T(4,128)(2,1)} %param.9) | non-fusion elementwise | flops 512 | bytes 3072 | tf_op jit(solution)/shard_map/convert_element_type | solution.py:385
  0.7 1.3 %select_reduce_fusion.wt_ref = f32[8,128]{1,0:T(8,128)} fusion(f32[128,4]{0,1:T(4,128)S(1)} %convert_element_type.3, s32[128,4]{0,1:T(4,128)} %param.8), kind=kLoop, calls=%fused_computation | loop fusion | flops 11264 | bytes 8192 | tf_op jit(solution)/shard_map/reduce_sum | solution.py:385
  2.0 58.0 %shard_map.55 = (bf16[4,128,4096]{2,1,0:T(8,128)(2,1)}, f32[4,8,128]{2,1,0:T(8,128)}) custom-call(f32[8,128]{1,0:T(8,128)} %select_reduce_fusion.wt_ref, bf16[128,4096]{1,0:T(8,128)(2,1)} %q_hbm.1, bf16[128,1024]{1,0:T(8,128)(2,1)} %k_hbm.1, bf16[128,1024]{1,0:T(8,128)(2,1)} %v_hbm.1), custom_call_target="tpu_custom_call" | custom-call | tf_op jit(solution)/shard_map/pallas_call | solution.py:314
  60.0 6.8 %shard_map.56 = bf16[2,1,4,96,4096]{4,3,2,1,0:T(8,128)(2,1)} custom-call(bf16[4,128,4096]{2,1,0:T(8,128)(2,1)} %get-tuple-element.7.att_ref, f32[4,8,128]{2,1,0:T(8,128)} %get-tuple-element.8.wt_ref), custom_call_target="tpu_custom_call" | custom-call | tf_op jit(solution)/shard_map/pallas_call | solution.py:368

commit v3 on v2

--- a/solution.py
+++ b/solution.py
@@ -83,6 +83,10 @@
         ref = kv.at[c, :, span_of(line, 2 * rows), :]
         return remote(ref, ref, z_send.at[c, line], z_recv.at[c, line], n, s + 2)
 
+    def z_part(c, j):
+        ref = kv.at[c, :, span_of(j, rows), :]
+        return remote(ref, ref, z_send.at[c, a], z_recv.at[c, a], n, s + 2)
+
     def z_arrived(c, line):
         ref = kv.at[c, :, span_of(line, 2 * rows), :]
         remote(ref, ref, z_send.at[c, line], z_recv.at[c, line], n, beside).wait_recv()
@@ -125,16 +129,25 @@
         kv_give(c, 1).start()
 
     loop(give_kv)
+
+    def own_out(c):
+        for which in range(2):
+            kv_keep(c, which).wait()
+
+        @pl.when(a < depth - 1)
+        def _():
+            z_part(c, s).start()
+
+    loop(own_out)
     loop(lambda c: q_give(c).start())
 
     def pair_out(c):
         for which in range(2):
-            kv_keep(c, which).wait()
             kv_taken(c, which).wait_recv()
 
         @pl.when(a < depth - 1)
         def _():
-            z_copy(c, a).start()
+            z_part(c, beside).start()
 
     def forward(c, send):
         for lag in range(1, depth):
@@ -350,17 +363,21 @@
     )
     earlier = earlier.astype(jnp.float32).astype(jnp.bfloat16)
     slots = lax.broadcasted_iota(jnp.int32, (cap, rows), 0).astype(jnp.float32)
+    tables = []
     for e in range(EXP_NODE):
         weight = jnp.broadcast_to(wt_ref[0, pl.ds(first + e, 1), :], (8, rows))
         member = jnp.where(weight > 0, jnp.float32(1.0), jnp.float32(0.0))
         rank = jnp.dot(member.astype(jnp.bfloat16), earlier, preferred_element_type=jnp.float32)
         gate = jnp.broadcast_to(weight[:1], (cap, rows))
         place = jnp.broadcast_to(rank[:1], (cap, rows))
-        table = jnp.where((gate > 0) & (place == slots), gate, 0.0).astype(jnp.bfloat16)
-        for at in range(0, width, 1024):
-            out_ref[e, 0, 0, :, at : at + 1024] = jnp.dot(
-                table, att_ref[0, :, at : at + 1024], preferred_element_type=jnp.float32
-            ).astype(jnp.bfloat16)
+        tables.append(jnp.where((gate > 0) & (place == slots), gate, 0.0).astype(jnp.bfloat16))
+    table = jnp.concatenate(tables, axis=0)
+    for at in range(0, width, 512):
+        rows_out = jnp.dot(
+            table, att_ref[0, :, at : at + 512], preferred_element_type=jnp.float32
+        ).astype(jnp.bfloat16)
+        for e in range(EXP_NODE):
+            out_ref[e, 0, 0, :, at : at + 512] = rows_out[e * cap : (e + 1) * cap]
 
 
 def pick(cap, att, wts):

time: 67 us -> 63.4 us (0.946)
  Pallas kernels: 64.8 us -> 60.7 us
    pallas_call x1, Pallas kernels: 58 us -> 54.2 us  [attend(): pl.pallas_call(functools.partial(attend_kernel, n_node, n_seq, rows), out...]
where the time goes in v3:
time: 63.4 us; the launch traced here: 62.7 us
  Pallas kernels  60.7 us (96%)
  other arithmetic  1.96 us (3%)
    pallas_call x1, Pallas kernels, attend(): pl.pallas_call(functools.partial(attend_kernel, n_node, n_seq, rows), out...  54.2 us
    pallas_call x1, Pallas kernels, pick(): pl.pallas_call(functools.partial(pick_kernel, cap), grid=(n_node,), out_s...  6.5 us
    reduce_sum x1, other arithmetic, per_device(): jnp.sum(jnp.where(match, gates.astype(jnp.float32)[None], jnp.float32(0.0...  1.28 us

profile of v3, /device:TPU:25, one launch (start us, length us, event | category | flops | bytes accessed | tf_op | source)
XLA Modules:
  0.0 62.7 jit_solution(11202857601255449526)
XLA Ops:
  0.0 0.7 %convert_element_type.3 = f32[128,4]{0,1:T(4,128)S(1)} convert(bf16[128,4]{0,1:T(4,128)(2,1)} %param.9) | non-fusion elementwise | flops 512 | bytes 3072 | tf_op jit(solution)/shard_map/convert_element_type | solution.py:402
  0.7 1.3 %select_reduce_fusion.wt_ref = f32[8,128]{1,0:T(8,128)} fusion(f32[128,4]{0,1:T(4,128)S(1)} %convert_element_type.3, s32[128,4]{0,1:T(4,128)} %param.8), kind=kLoop, calls=%fused_computation | loop fusion | flops 11264 | bytes 8192 | tf_op jit(solution)/shard_map/reduce_sum | solution.py:402
  2.0 54.2 %shard_map.55 = (bf16[4,128,4096]{2,1,0:T(8,128)(2,1)}, f32[4,8,128]{2,1,0:T(8,128)}) custom-call(f32[8,128]{1,0:T(8,128)} %select_reduce_fusion.wt_ref, bf16[128,4096]{1,0:T(8,128)(2,1)} %q_hbm.1, bf16[128,1024]{1,0:T(8,128)(2,1)} %k_hbm.1, bf16[128,1024]{1,0:T(8,128)(2,1)} %v_hbm.1), custom_call_target="tpu_custom_call" | custom-call | tf_op jit(solution)/shard_map/pallas_call | solution.py:327
  56.2 6.5 %shard_map.56 = bf16[2,1,4,96,4096]{4,3,2,1,0:T(8,128)(2,1)} custom-call(bf16[4,128,4096]{2,1,0:T(8,128)(2,1)} %get-tuple-element.7.att_ref, f32[4,8,128]{2,1,0:T(8,128)} %get-tuple-element.8.wt_ref), custom_call_target="tpu_custom_call" | custom-call | tf_op jit(solution)/shard_map/pallas_call | solution.py:385

commit v4 on v3

--- a/solution.py
+++ b/solution.py
@@ -139,7 +139,7 @@
             z_part(c, s).start()
 
     loop(own_out)
-    loop(lambda c: q_give(c).start())
+    q_give(0).start()
 
     def pair_out(c):
         for which in range(2):
@@ -266,6 +266,11 @@
             forward(c, False)
 
         q_taken(c).wait_recv()
+
+        @pl.when(c + 1 < steps)
+        def _():
+            q_give(c + 1).start()
+
         compute(c, 1 - b)
         x_give(c).start()
 
@@ -281,10 +286,14 @@
         @pl.when(c > 0)
         def _():
             att_forward(b, c - 1)
-            att_forward(1 - b, c - 1)
+
+        @pl.when(c > 1)
+        def _():
+            att_forward(1 - b, c - 2)
 
     loop(step)
     relay(steps - 1)
+    att_forward(1 - b, steps - 2)
     att_forward(b, steps - 1)
     att_forward(1 - b, steps - 1)
 
@@ -363,34 +372,35 @@
     )
     earlier = earlier.astype(jnp.float32).astype(jnp.bfloat16)
     slots = lax.broadcasted_iota(jnp.int32, (cap, rows), 0).astype(jnp.float32)
-    tables = []
-    for e in range(EXP_NODE):
-        weight = jnp.broadcast_to(wt_ref[0, pl.ds(first + e, 1), :], (8, rows))
-        member = jnp.where(weight > 0, jnp.float32(1.0), jnp.float32(0.0))
-        rank = jnp.dot(member.astype(jnp.bfloat16), earlier, preferred_element_type=jnp.float32)
-        gate = jnp.broadcast_to(weight[:1], (cap, rows))
-        place = jnp.broadcast_to(rank[:1], (cap, rows))
-        tables.append(jnp.where((gate > 0) & (place == slots), gate, 0.0).astype(jnp.bfloat16))
-    table = jnp.concatenate(tables, axis=0)
-    for at in range(0, width, 512):
-        rows_out = jnp.dot(
-            table, att_ref[0, :, at : at + 512], preferred_element_type=jnp.float32
-        ).astype(jnp.bfloat16)
+    for m in range(att_ref.shape[0]):
+        tables = []
         for e in range(EXP_NODE):
-            out_ref[e, 0, 0, :, at : at + 512] = rows_out[e * cap : (e + 1) * cap]
+            weight = jnp.broadcast_to(wt_ref[m, pl.ds(first + e, 1), :], (8, rows))
+            member = jnp.where(weight > 0, jnp.float32(1.0), jnp.float32(0.0))
+            rank = jnp.dot(member.astype(jnp.bfloat16), earlier, preferred_element_type=jnp.float32)
+            gate = jnp.broadcast_to(weight[:1], (cap, rows))
+            place = jnp.broadcast_to(rank[:1], (cap, rows))
+            tables.append(jnp.where((gate > 0) & (place == slots), gate, 0.0).astype(jnp.bfloat16))
+        table = jnp.concatenate(tables, axis=0)
+        for at in range(0, width, 512):
+            rows_out = jnp.dot(
+                table, att_ref[m, :, at : at + 512], preferred_element_type=jnp.float32
+            ).astype(jnp.bfloat16)
+            for e in range(EXP_NODE):
+                out_ref[e, 0, m, :, at : at + 512] = rows_out[e * cap : (e + 1) * cap]
 
 
 def pick(cap, att, wts):
     n_node, rows, width = att.shape
     return pl.pallas_call(
         functools.partial(pick_kernel, cap),
-        grid=(n_node,),
+        grid=(n_node // 2,),
         out_shape=jax.ShapeDtypeStruct((EXP_NODE, 1, n_node, cap, width), jnp.bfloat16),
         in_specs=[
-            pl.BlockSpec((1, rows, width), lambda i: (i, 0, 0)),
-            pl.BlockSpec((1,) + wts.shape[1:], lambda i: (i, 0, 0)),
+            pl.BlockSpec((2, rows, width), lambda i: (i, 0, 0)),
+            pl.BlockSpec((2,) + wts.shape[1:], lambda i: (i, 0, 0)),
         ],
-        out_specs=pl.BlockSpec((EXP_NODE, 1, 1, cap, width), lambda i: (0, 0, i, 0, 0)),
+        out_specs=pl.BlockSpec((EXP_NODE, 1, 2, cap, width), lambda i: (0, 0, i, 0, 0)),
         compiler_params=pltpu.CompilerParams(vmem_limit_bytes=60 * 1024 * 1024),
     )(att, wts)
 

time: 63.4 us -> 61.4 us (0.968)
  Pallas kernels: 60.7 us -> 59.2 us
    pallas_call x1, Pallas kernels: 6.5 us -> 5.74 us  [pick(): pl.pallas_call(functools.partial(pick_kernel, cap), grid=(n_node // 2,),...]
    pallas_call x1, Pallas kernels: 54.2 us -> 53.4 us  [attend(): pl.pallas_call(functools.partial(attend_kernel, n_node, n_seq, rows), out...]
where the time goes in v4:
time: 61.4 us; the launch traced here: 61.2 us
  Pallas kernels  59.2 us (96%)
  other arithmetic  1.96 us (3%)
    pallas_call x1, Pallas kernels, attend(): pl.pallas_call(functools.partial(attend_kernel, n_node, n_seq, rows), out...  53.4 us
    pallas_call x1, Pallas kernels, pick(): pl.pallas_call(functools.partial(pick_kernel, cap), grid=(n_node // 2,),...  5.74 us
    reduce_sum x1, other arithmetic, per_device(): jnp.sum(jnp.where(match, gates.astype(jnp.float32)[None], jnp.float32(0.0...  1.28 us

profile of v4, /device:TPU:25, one launch (start us, length us, event | category | flops | bytes accessed | tf_op | source)
XLA Modules:
  0.0 61.2 jit_solution(3685341110897940325)
XLA Ops:
  0.0 0.7 %convert_element_type.3 = f32[128,4]{0,1:T(4,128)S(1)} convert(bf16[128,4]{0,1:T(4,128)(2,1)} %param.9) | non-fusion elementwise | flops 512 | bytes 3072 | tf_op jit(solution)/shard_map/convert_element_type | solution.py:412
  0.7 1.3 %select_reduce_fusion.wt_ref = f32[8,128]{1,0:T(8,128)} fusion(f32[128,4]{0,1:T(4,128)S(1)} %convert_element_type.3, s32[128,4]{0,1:T(4,128)} %param.8), kind=kLoop, calls=%fused_computation | loop fusion | flops 11264 | bytes 8192 | tf_op jit(solution)/shard_map/reduce_sum | solution.py:412
  2.0 53.4 %shard_map.55 = (bf16[4,128,4096]{2,1,0:T(8,128)(2,1)}, f32[4,8,128]{2,1,0:T(8,128)}) custom-call(f32[8,128]{1,0:T(8,128)} %select_reduce_fusion.wt_ref, bf16[128,4096]{1,0:T(8,128)(2,1)} %q_hbm.1, bf16[128,1024]{1,0:T(8,128)(2,1)} %k_hbm.1, bf16[128,1024]{1,0:T(8,128)(2,1)} %v_hbm.1), custom_call_target="tpu_custom_call" | custom-call | tf_op jit(solution)/shard_map/pallas_call | solution.py:336
  55.4 5.7 %shard_map.56 = bf16[2,1,4,96,4096]{4,3,2,1,0:T(8,128)(2,1)} custom-call(bf16[4,128,4096]{2,1,0:T(8,128)(2,1)} %get-tuple-element.7.att_ref, f32[4,8,128]{2,1,0:T(8,128)} %get-tuple-element.8.wt_ref), custom_call_target="tpu_custom_call" | custom-call | tf_op jit(solution)/shard_map/pallas_call | solution.py:395
